TPU v7x, 32 devices: a whole 2x2x4 slice. The times are simulated.
32 devices in a mesh: groups: 2 (over y), batch: 4 (over z), mp: 4 (over x, core).
Axes of the slice: x: 2, y: 2, z: 4, core: 2. Of those that a mesh axis runs over, the one named last changes fastest.
Arguments:
- tokens: bfloat16 [192, 18432], P(('groups', 'batch'), 'mp'), parts along dimension 0, may hold values from -3000 to 3000
- norm_gain: float32 [18432], P('mp'), may hold values from 0.1 to 1.9
- w_qkv: bfloat16 [18432, 12800], P('mp', 'batch'), may hold values from -0.046875 to 0.046875
- key_cache: bfloat16 [192, 512, 256], P(('groups', 'batch', 'mp')), parts along dimension 0, may hold values from -200 to 200
- value_cache: bfloat16 [192, 512, 256], P(('groups', 'batch', 'mp')), parts along dimension 0, may hold values from -6 to 6
- lengths: int32 [192], P(('groups', 'batch', 'mp')), parts along dimension 0, may hold values from 1 to 512, as said below
Outputs:
- context: bfloat16 [192, 12288], P(('groups', 'batch', 'mp')), parts along dimension 0
There are 2 independent parts, one for each index of `groups`. A program takes and returns all parts, laid end to end along the dimension named above; an argument that names none is the same for every part. Nothing has to cross between parts.
Inputs may be any that keep to these rules, and one draw needn't show every extreme that they name: `lengths`: some row uses all 512 positions and some row uses one.
All inputs are finite; a program needn't handle non-finite values.
Results may differ from a plain program's by a relative error of at most 0.0033.
The roundings to bfloat16 on the way count: a program that leaves them out, or rounds other values in their place, can miss the bound.
Values may be sent and summed in bfloat16 or wider, within the bound.
A program may use at most 128 MiB of HBM per device.

v0:
```python
import math

import jax
import jax.numpy as jnp
from jax import lax
from jax.sharding import PartitionSpec as P

D = 18432
HQ = 48
HD = 256


EPSILON = 1e-06
NEG_FILL = -1e30


def attend(raw_qkv, inv_rms, key_cache, value_cache, lengths):
    row_count = raw_qkv.shape[0]
    queries = raw_qkv[:, : HQ * HD].reshape(row_count, HQ, HD)
    new_key = raw_qkv[:, HQ * HD : HQ * HD + HD]
    new_value = raw_qkv[:, HQ * HD + HD :]
    scale = inv_rms[:, None, None] / math.sqrt(HD)
    scores = (
        jnp.einsum("rhd,rpd->rhp", queries, key_cache, preferred_element_type=jnp.float32) * scale
    )
    own_score = (
        jnp.einsum("rhd,rd->rh", queries, new_key, preferred_element_type=jnp.float32)
        * (inv_rms * inv_rms / math.sqrt(HD))[:, None]
    )
    positions = jnp.arange(key_cache.shape[1], dtype=jnp.int32)
    valid_mask = (positions[None, :] < lengths[:, None])[:, None, :]
    scores = jnp.where(valid_mask, scores, NEG_FILL)
    row_max = jnp.maximum(jnp.max(scores, axis=2), own_score)
    weights = jnp.where(valid_mask, jnp.exp(scores - row_max[:, :, None]), 0.0)
    own_weight = jnp.exp(own_score - row_max)
    denominator = jnp.sum(weights, axis=2) + own_weight
    weights_low = weights.astype(jnp.bfloat16)
    weighted = jnp.einsum(
        "rhp,rpd->rhd", weights_low, value_cache, preferred_element_type=jnp.float32
    )
    weighted = (
        weighted
        + own_weight[:, :, None]
        * inv_rms[:, None, None]
        * new_value.astype(jnp.float32)[:, None, :]
    )
    context = weighted / denominator[:, :, None]
    return context.astype(jnp.bfloat16).reshape(row_count, HQ * HD)


def per_device(tokens, norm_gain, w_qkv, key_cache, value_cache, lengths):
    widened = tokens.astype(jnp.float32)
    normed = (widened * norm_gain).astype(jnp.bfloat16)
    square_part = jnp.sum(widened * widened, axis=1)
    partial_value = jnp.dot(
        lax.all_gather(normed, "batch", axis=0, tiled=True),
        w_qkv,
        preferred_element_type=jnp.float32,
    )
    batch_count = lax.axis_size("batch")
    model_count = lax.axis_size("mp")
    row_total = tokens.shape[0]
    row_share = row_total // model_count
    col_width = w_qkv.shape[1]
    blocks = partial_value.reshape(batch_count, model_count, row_share, col_width)
    summed, square_sum = (
        lax.psum_scatter(blocks, "mp", scatter_dimension=1, tiled=True),
        lax.psum_scatter(
            square_part.reshape(1, model_count, row_share), "mp", scatter_dimension=1, tiled=True
        ),
    )
    arrived = lax.all_to_all(
        summed.astype(jnp.bfloat16), "batch", split_axis=0, concat_axis=3, tiled=True
    )
    raw_qkv = arrived.reshape(row_share, batch_count * col_width)
    square_sum = square_sum.reshape(row_share)
    inv_rms = 1.0 / jnp.sqrt(square_sum / D + EPSILON)
    return attend(raw_qkv, inv_rms, key_cache, value_cache, lengths)


def solution(mesh):
    return jax.shard_map(
        per_device,
        mesh=mesh,
        in_specs=(
            P(("groups", "batch"), "mp"),
            P("mp"),
            P("mp", "batch"),
            P(("groups", "batch", "mp"), None, None),
            P(("groups", "batch", "mp"), None, None),
            P(("groups", "batch", "mp")),
        ),
        out_specs=P(("groups", "batch", "mp"), None),
        check_vma=False,
    )
```

profile of v0, /device:TPU:0, one launch (start us, length us, event | category | flops | bytes accessed | tf_op | source)
XLA Modules:
  0.0 84.1 jit_solution(15100001956926033296)
XLA Ops:
  0.0 0.0 copy-start
  0.0 1.2 %fusion.6 = (bf16[24,4608]{1,0:T(8,128)(2,1)S(1)}, f32[24]{0:T(128)S(1)}) fusion(bf16[24,4608]{1,0:T(8,128)(2,1)} %param.6, f32[4608]{0:T(1024)} %param.7), kind=kLoop, calls=%fused_computation.11 | loop fusion | flops 552936 | bytes 460896 | tf_op jit(solution)/shard_map/convert_element_type | solution.py:53
  1.2 22.4 %all_gather.3 = bf16[96,4608]{1,0:T(8,128)(2,1)S(1)} all-gather(bf16[24,4608]{1,0:T(8,128)(2,1)S(1)} %get-tuple-element.9), channel_id=1, replica_groups=mesh['groups'=2,'batch'=4,'mp'=4] {'batch'}, dimensions={0}, use_global_device_ids=true | all-gather | bytes 1105920 | tf_op jit(solution)/shard_map/all_gather | solution.py:56
  23.6 12.9 %fusion.26 = f32[96,3200]{1,0:T(8,128)} fusion(bf16[96,4608]{1,0:T(8,128)(2,1)S(1)} %all_gather.3, bf16[4608,3200]{1,0:T(8,128)(2,1)} %param.8), kind=kOutput, calls=%fused_computation.40 | convolution fusion | flops 2831155200 | bytes 31604736 | tf_op jit(solution)/shard_map/dot_general | solution.py:55
  36.5 1.4 %reshape.68 = f32[4,4,6,3200]{3,2,1,0:T(8,128)S(1)} reshape(f32[96,3200]{1,0:T(8,128)} %fusion.26) | data formatting | bytes 2457600 | tf_op jit(solution)/shard_map/reshape | solution.py:65
  37.9 0.0 copy-start.3
  37.9 1.8 %copy.8 = f32[4,4,6,3200]{3,0,2,1:T(4,128)} copy(f32[4,4,6,3200]{3,2,1,0:T(8,128)S(1)} %reshape.68) | data formatting | bytes 2457600 | tf_op jit(solution)/shard_map/reshape | solution.py:65
  39.7 0.0 copy-start.1
  39.7 0.1 reshape.71
  39.8 27.7 %all-reduce.4 = (f32[1,4,6]{2,1,0:T(4,128)S(1)}, bf16[4,4,6,3200]{3,0,2,1:T(4,128)(2,1)S(1)}) all-reduce(f32[1,4,6]{2,1,0:T(4,128)S(1)} %reshape.71, f32[4,4,6,3200]{3,0,2,1:T(4,128)} %copy.8), channel_id=3, replica_groups=mesh['groups'=2,'batch'=4,'mp'=4] {'mp'}, use_global_device_ids=true, to_apply=%region_2.0.clone | all-reduce | flops 307224 | bytes 1843392
  67.6 0.0 copy-done.3
  67.6 0.6 dynamic-slice
  68.2 0.7 dynamic-slice_convert_fusion
  68.9 0.7 copy.9
  69.6 3.4 %all-to-all-start = ((bf16[4,1,6,3200]{3,2,1,0:T(8,128)(2,1)}), bf16[4,1,6,3200]{3,2,1,0:T(8,128)(2,1)S(1)}, u32[]{:S(2)}, u32[]{:S(2)}) async-start(bf16[4,1,6,3200]{3,2,1,0:T(8,128)(2,1)} %copy.9), calls=%async_computation | async-start | bytes 409600 | tf_op jit(solution)/shard_map/all_to_all | solution.py:72
  73.0 0.7 multiply_multiply_fusion
  73.6 0.0 copy-done.1
  73.6 0.1 iota_compare_fusion
  73.7 7.8 %all-to-all-done = bf16[4,1,6,3200]{3,2,1,0:T(8,128)(2,1)S(1)} async-done(((bf16[4,1,6,3200]{3,2,1,0:T(8,128)(2,1)}), bf16[4,1,6,3200]{3,2,1,0:T(8,128)(2,1)S(1)}, u32[]{:S(2)}, u32[]{:S(2)}) %all-to-all-start) | async-done | bytes 153632 | tf_op jit(solution)/shard_map/all_to_all | solution.py:72
  81.5 0.0 copy-start.2
  81.5 0.1 fusion.12
  81.6 0.0 copy-done
  81.7 0.7 fusion.25
  82.3 0.1 fusion.19
  82.4 0.2 fusion.4
  82.6 0.1 broadcast_multiply_fusion
  82.7 0.2 copy-done.2
  82.9 0.4 fusion.3
  83.4 0.7 copy.15
  (3 shorter events, 0.0 us)
Async XLA Ops:
  0.0 81.7 %copy-start = (bf16[6,512,256]{2,1,0:T(8,128)(2,1)S(1)}, bf16[6,512,256]{2,1,0:T(8,128)(2,1)}, u32[]{:S(2)}) copy-start(bf16[6,512,256]{2,1,0:T(8,128)(2,1)} %param.9) | copy-start | bytes 4718596
  37.9 29.7 %copy-start.3 = (u32[32]{0:T(128)S(1)}, u32[32]{0:T(128)}, u32[]{:S(2)}) copy-start(u32[32]{0:T(128)} %constant.22) | copy-start | bytes 388
  39.7 33.9 %copy-start.1 = (s32[6]{0:T(128)S(1)}, s32[6]{0:T(128)}, u32[]{:S(2)}) copy-start(s32[6]{0:T(128)} %param.11) | copy-start | bytes 76
  69.6 11.9 %all-to-all-start = ((bf16[4,1,6,3200]{3,2,1,0:T(8,128)(2,1)}), bf16[4,1,6,3200]{3,2,1,0:T(8,128)(2,1)S(1)}, u32[]{:S(2)}, u32[]{:S(2)}) async-start(bf16[4,1,6,3200]{3,2,1,0:T(8,128)(2,1)} %copy.9), calls=%async_computation | async-start | bytes 409600 | tf_op jit(solution)/shard_map/all_to_all | solution.py:72
  81.5 1.4 %copy-start.2 = (bf16[6,512,256]{2,1,0:T(8,128)(2,1)S(1)}, bf16[6,512,256]{2,1,0:T(8,128)(2,1)}, u32[]{:S(2)}) copy-start(bf16[6,512,256]{2,1,0:T(8,128)(2,1)} %param.10) | copy-start | bytes 4718596
where the time goes:
time: 84.4 us; the launch traced here: 84.1 us
  blocking collectives  50.1 us (59%)
  matrix products  14.1 us (17%)
  waiting for transfers between devices  7.75 us (9%)
  local copies, waits for them, and re-layouts  6.21 us (7%)
  starting transfers between devices  3.37 us (4%)
  other arithmetic  2.37 us (3%)
    unnamed x1, blocking collectives  27.7 us
    all_gather x1, blocking collectives, per_device(): lax.all_gather(normed, 'batch', axis=0, tiled=True)  22.4 us
    dot_general x1, matrix products, per_device(): jnp.dot(lax.all_gather(normed, 'batch', axis=0, tiled=True), w_qkv, prefe...  12.9 us
    all_to_all x1, waiting for transfers between devices, per_device(): lax.all_to_all(summed.astype(jnp.bfloat16), 'batch', split_axis=0, concat...  7.75 us
    all_to_all x1, starting transfers between devices, per_device(): lax.all_to_all(summed.astype(jnp.bfloat16), 'batch', split_axis=0, concat...  3.37 us
    reshape x2, local copies, waits for them, and re-layouts, per_device(): partial_value.reshape(batch_count, model_count, row_share, col_width)  3.21 us
  transfers between devices with their start and end apart: 1, of which 1 were waited for; matrix products, arithmetic and copies ran while one was open for 1% of the time, Pallas kernels for 0%

commit v1 on v0

--- a/solution.py
+++ b/solution.py
@@ -3,6 +3,8 @@
 import jax
 import jax.numpy as jnp
 from jax import lax
+from jax.experimental import pallas as pl
+from jax.experimental.pallas import tpu as pltpu
 from jax.sharding import PartitionSpec as P
 
 D = 18432
@@ -12,6 +14,19 @@
 
 EPSILON = 1e-06
 NEG_FILL = -1e30
+
+BATCH = 4
+MODEL = 4
+ROWS = 24
+SHARE = 6
+HALF = 256
+CHUNK = 2 * HALF
+LANES = 128
+PIECE = 5
+PIECE_COLS = PIECE * LANES
+PIECE_ROWS = 32
+HEAD_ROWS = 64
+MESH_ID = pl.DeviceIdType.MESH
 
 
 def attend(raw_qkv, inv_rms, key_cache, value_cache, lengths):
@@ -48,7 +63,7 @@
     return context.astype(jnp.bfloat16).reshape(row_count, HQ * HD)
 
 
-def per_device(tokens, norm_gain, w_qkv, key_cache, value_cache, lengths):
+def plain_device(tokens, norm_gain, w_qkv, key_cache, value_cache, lengths):
     widened = tokens.astype(jnp.float32)
     normed = (widened * norm_gain).astype(jnp.bfloat16)
     square_part = jnp.sum(widened * widened, axis=1)
@@ -76,6 +91,375 @@
     square_sum = square_sum.reshape(row_share)
     inv_rms = 1.0 / jnp.sqrt(square_sum / D + EPSILON)
     return attend(raw_qkv, inv_rms, key_cache, value_cache, lengths)
+
+
+def one_hot(source, width):
+    lanes = lax.broadcasted_iota(jnp.int32, (source.shape[0], width), 1)
+    return jnp.where(lanes == source, 1.0, 0.0).astype(jnp.bfloat16)
+
+
+def row_index(count):
+    return lax.broadcasted_iota(jnp.int32, (count, 1), 0)
+
+
+def gather_matrix():
+    index = row_index(2 * BATCH * ROWS)
+    half = lax.div(index, BATCH * ROWS)
+    place = lax.rem(index, BATCH * ROWS)
+    core = lax.div(place, 2 * ROWS)
+    along_x = lax.rem(lax.div(place, ROWS), 2)
+    batch = lax.div(lax.rem(place, ROWS), SHARE)
+    row = lax.rem(place, SHARE)
+    source = batch * (2 * ROWS) + half * ROWS + (along_x * 2 + core) * SHARE + row
+    return one_hot(source, 2 * BATCH * ROWS)
+
+
+def scatter_matrix():
+    index = row_index(BATCH * PIECE_ROWS)
+    batch = lax.div(index, PIECE_ROWS)
+    within = lax.rem(index, PIECE_ROWS)
+    block = lax.div(within, SHARE)
+    row = lax.rem(within, SHARE)
+    source = jnp.where(within < PIECE * SHARE, block * ROWS + batch * SHARE + row, -1)
+    return one_hot(source, LANES)
+
+
+def head_matrix(row, width):
+    index = row_index(2 * HEAD_ROWS)
+    half = lax.div(index, HEAD_ROWS)
+    head = lax.rem(index, HEAD_ROWS)
+    block = head * 2 + half
+    piece = lax.div(block, PIECE)
+    source = piece * PIECE_ROWS + (block - piece * PIECE) * SHARE + row
+    return one_hot(source, width)
+
+
+def fused_kernel(
+    lengths_ref, tokens_ref, gain_ref, w_ref, key_ref, value_ref, out_ref,
+    w_buf, key_buf, value_buf, gathered, order, spread, heads, acc,
+    core_in, x_out, x_in, z_out, z_in, squares, inverse,
+    w_sem, cache_sem,
+    right_send, right_recv, left_send, left_recv,
+    core_send, core_recv, x_send, x_recv, z_send, z_recv, sq_send, sq_recv,
+):
+    group = lax.axis_index("groups")
+    batch = lax.axis_index("batch")
+    model = lax.axis_index("mp")
+    core = lax.rem(model, 2)
+    along_x = lax.div(model, 2)
+    sibling = model + 1 - 2 * core
+    across = lax.rem(model + 2, MODEL)
+    chunks = w_ref.shape[0] // CHUNK
+    pieces = w_ref.shape[1] // PIECE_COLS
+
+    barrier = pltpu.get_barrier_semaphore()
+    for step in range(1, BATCH):
+        pl.semaphore_signal(
+            barrier, inc=1, device_id=(group, lax.rem(batch + step, BATCH), model),
+            device_id_type=MESH_ID,
+        )
+    for step in range(1, MODEL):
+        pl.semaphore_signal(
+            barrier, inc=1, device_id=(group, batch, lax.rem(model + step, MODEL)),
+            device_id_type=MESH_ID,
+        )
+
+    def w_copy(k):
+        return pltpu.make_async_copy(
+            w_ref.at[pl.ds(pl.multiple_of(k * CHUNK, CHUNK), CHUNK)], w_buf.at[k], w_sem.at[k]
+        )
+
+    @pl.loop(0, chunks)
+    def _(k):
+        w_copy(k).start()
+
+    key_copy = pltpu.make_async_copy(key_ref, key_buf, cache_sem.at[0])
+    value_copy = pltpu.make_async_copy(value_ref, value_buf, cache_sem.at[1])
+    key_copy.start()
+    value_copy.start()
+
+    total = jnp.zeros((ROWS, LANES), jnp.float32)
+    for k in range(chunks):
+        parts = []
+        for half in range(2):
+            columns = pl.ds(k * CHUNK + half * HALF, HALF)
+            widened = tokens_ref[:, columns].astype(jnp.float32)
+            parts.append(widened * gain_ref[:, columns])
+            squared = widened * widened
+            total = total + squared[:, :LANES] + squared[:, LANES:]
+        gathered[k, batch] = jnp.concatenate(parts, axis=0).astype(jnp.bfloat16)
+    squares[model] = jnp.broadcast_to(jnp.sum(total, axis=1, keepdims=True), (ROWS, LANES))
+
+    pl.semaphore_wait(barrier, BATCH + MODEL - 2)
+
+    def to_right(d, k):
+        block = gathered.at[k, lax.max(batch - d, 0)]
+        return pltpu.make_async_remote_copy(
+            src_ref=block, dst_ref=block,
+            send_sem=right_send.at[d, k], recv_sem=right_recv.at[d, k],
+            device_id=(group, lax.min(batch + 1, BATCH - 1), model), device_id_type=MESH_ID,
+        )
+
+    def to_left(d, k):
+        block = gathered.at[k, lax.min(batch + d, BATCH - 1)]
+        return pltpu.make_async_remote_copy(
+            src_ref=block, dst_ref=block,
+            send_sem=left_send.at[d, k], recv_sem=left_recv.at[d, k],
+            device_id=(group, lax.max(batch - 1, 0), model), device_id_type=MESH_ID,
+        )
+
+    def sends_right(d):
+        return jnp.logical_and(batch >= d, batch < BATCH - 1)
+
+    def sends_left(d):
+        return jnp.logical_and(batch + d < BATCH, batch > 0)
+
+    def send(d, k):
+        pl.when(sends_right(d))(lambda: to_right(d, k).start())
+        pl.when(sends_left(d))(lambda: to_left(d, k).start())
+
+    def receive(d, k):
+        incoming = gathered.at[k, 0]
+
+        @pl.when(batch >= d + 1)
+        def _():
+            pltpu.make_async_remote_copy(
+                src_ref=incoming, dst_ref=gathered.at[k, lax.max(batch - d - 1, 0)],
+                send_sem=right_send.at[d, k], recv_sem=right_recv.at[d, k],
+                device_id=(group, lax.max(batch - 1, 0), model), device_id_type=MESH_ID,
+            ).wait_recv()
+            if d + 1 < BATCH - 1:
+                pl.when(batch < BATCH - 1)(lambda: to_right(d + 1, k).start())
+
+        @pl.when(batch + d + 1 < BATCH)
+        def _():
+            pltpu.make_async_remote_copy(
+                src_ref=incoming, dst_ref=gathered.at[k, lax.min(batch + d + 1, BATCH - 1)],
+                send_sem=left_send.at[d, k], recv_sem=left_recv.at[d, k],
+                device_id=(group, lax.min(batch + 1, BATCH - 1), model), device_id_type=MESH_ID,
+            ).wait_recv()
+            if d + 1 < BATCH - 1:
+                pl.when(batch > 0)(lambda: to_left(d + 1, k).start())
+
+    send(0, 0)
+    send(0, 1)
+
+    def square_copy(step):
+        return pltpu.make_async_remote_copy(
+            src_ref=squares.at[model], dst_ref=squares.at[model],
+            send_sem=sq_send.at[step], recv_sem=sq_recv.at[step],
+            device_id=(group, batch, lax.rem(model + step, MODEL)), device_id_type=MESH_ID,
+        )
+
+    for step in range(1, MODEL):
+        square_copy(step).start()
+
+    order[...] = gather_matrix()
+    spread[...] = scatter_matrix()
+    for row in range(SHARE):
+        heads[row] = head_matrix(row, heads.shape[2])
+
+    def left_side(k):
+        arrived = gathered[k].reshape(2 * BATCH * ROWS, HALF)
+        ordered = jnp.dot(order[...], arrived, preferred_element_type=jnp.float32)
+        ordered = ordered.astype(jnp.bfloat16)
+        return jnp.concatenate([ordered[: BATCH * ROWS], ordered[BATCH * ROWS :]], axis=1)
+
+    acc[...] = jnp.zeros_like(acc)
+
+    width = w_ref.shape[1]
+    tile = 3 * HD
+
+    @pl.loop(0, chunks + 1)
+    def _(it):
+        pl.when(it + 2 < chunks)(lambda: send(0, it + 2))
+        pl.when(it < chunks)(lambda: receive(0, it))
+        pl.when(jnp.logical_and(it >= 1, it < chunks + 1))(lambda: receive(1, it - 1))
+
+        @pl.when(it >= 2)
+        def _():
+            k = it - 2
+            receive(2, k)
+            w_copy(k).wait()
+            left = left_side(k)
+            start = 0
+            while start < width:
+                stop = width if width - start < 2 * tile - LANES else start + tile
+                acc[:, start:stop] += jnp.dot(
+                    left, w_buf[k, :, start:stop], preferred_element_type=jnp.float32
+                )
+                start = stop
+
+    last = chunks - 1
+    receive(2, last)
+    w_copy(last).wait()
+    left = left_side(last)
+
+    def half_rows(which):
+        return pl.ds(pl.multiple_of(which * (2 * ROWS), 8), 2 * ROWS)
+
+    def core_copy(j):
+        return pltpu.make_async_remote_copy(
+            src_ref=acc.at[half_rows(1 - core), pl.ds(j * PIECE_COLS, PIECE_COLS)],
+            dst_ref=core_in.at[j],
+            send_sem=core_send.at[j], recv_sem=core_recv.at[j],
+            device_id=(group, batch, sibling), device_id_type=MESH_ID,
+        )
+
+    def x_copy(j):
+        return pltpu.make_async_remote_copy(
+            src_ref=x_out.at[j], dst_ref=x_in.at[j],
+            send_sem=x_send.at[j], recv_sem=x_recv.at[j],
+            device_id=(group, batch, across), device_id_type=MESH_ID,
+        )
+
+    def z_copy(j, step):
+        other = lax.rem(batch + step, BATCH)
+        return pltpu.make_async_remote_copy(
+            src_ref=z_out.at[j, other], dst_ref=z_in.at[batch, j],
+            send_sem=z_send.at[step, j], recv_sem=z_recv.at[step, j],
+            device_id=(group, other, model), device_id_type=MESH_ID,
+        )
+
+    def pair_sum(j, which):
+        rows = pl.ds(pl.multiple_of(core * (2 * ROWS) + which * ROWS, 8), ROWS)
+        own = acc[rows, pl.ds(j * PIECE_COLS, PIECE_COLS)]
+        return own + core_in[j, pl.ds(pl.multiple_of(which * ROWS, 8), ROWS)]
+
+    def pass_across(j):
+        core_copy(j).wait_recv()
+        x_out[j] = pair_sum(j, 1 - along_x)
+        x_copy(j).start()
+
+    for j in range(pieces):
+        columns = slice(j * PIECE_COLS, (j + 1) * PIECE_COLS)
+        acc[:, columns] += jnp.dot(
+            left, w_buf[last, :, columns], preferred_element_type=jnp.float32
+        )
+        core_copy(j).start()
+        if j:
+            pass_across(j - 1)
+    pass_across(pieces - 1)
+
+    for j in range(pieces):
+        x_copy(j).wait_recv()
+        final = pair_sum(j, along_x) + x_in[j]
+        blocks = [final[:, h * LANES : (h + 1) * LANES] for h in range(PIECE)]
+        blocks.append(jnp.zeros((LANES - PIECE * ROWS, LANES), jnp.float32))
+        stacked = jnp.concatenate(blocks, axis=0).astype(jnp.bfloat16)
+        placed = jnp.dot(spread[...], stacked, preferred_element_type=jnp.float32)
+        z_out[j] = placed.astype(jnp.bfloat16).reshape(BATCH, PIECE_ROWS, LANES)
+        for step in range(1, BATCH):
+            z_copy(j, step).start()
+        z_in[batch, j] = z_out[j, batch]
+
+    for step in range(1, MODEL):
+        square_copy(step).wait_recv()
+    square_sum = squares[0] + squares[1] + squares[2] + squares[3]
+    inverse[...] = 1.0 / jnp.sqrt(square_sum / D + EPSILON)
+    key_copy.wait()
+    value_copy.wait()
+    for j in range(pieces):
+        for step in range(1, BATCH):
+            z_copy(j, step).wait_recv()
+
+    columns = z_in[...].reshape(BATCH * pieces * PIECE_ROWS, LANES)
+    positions = lax.broadcasted_iota(jnp.int32, (HQ, key_ref.shape[1]), 1)
+    for row in range(SHARE):
+        picked = jnp.dot(heads[row], columns, preferred_element_type=jnp.float32)
+        joined = jnp.concatenate([picked[:HEAD_ROWS], picked[HEAD_ROWS:]], axis=1)
+        queries = joined[:HQ]
+        new_key = joined[HQ : HQ + 1]
+        new_value = joined[HQ + 1 : HQ + 2]
+        inv_rms = inverse[pl.ds(model * SHARE + row, 1), :][:, :1]
+        scores = lax.dot_general(
+            queries.astype(jnp.bfloat16), key_buf[row], (((1,), (1,)), ((), ())),
+            preferred_element_type=jnp.float32,
+        ) * (inv_rms / math.sqrt(HD))
+        own_score = jnp.sum(queries * new_key, axis=1, keepdims=True) * (
+            inv_rms * inv_rms / math.sqrt(HD)
+        )
+        valid = positions < lengths_ref[row]
+        scores = jnp.where(valid, scores, NEG_FILL)
+        row_max = jnp.maximum(jnp.max(scores, axis=1, keepdims=True), own_score)
+        weights = jnp.where(valid, jnp.exp(scores - row_max), 0.0)
+        own_weight = jnp.exp(own_score - row_max)
+        denominator = jnp.sum(weights, axis=1, keepdims=True) + own_weight
+        weighted = jnp.dot(
+            weights.astype(jnp.bfloat16), value_buf[row], preferred_element_type=jnp.float32
+        )
+        weighted = weighted + own_weight * inv_rms * new_value
+        out_ref[row] = (weighted / denominator).astype(jnp.bfloat16)
+
+    @pl.loop(0, chunks)
+    def _(k):
+        for d in range(BATCH - 1):
+            pl.when(sends_right(d))(lambda d=d: to_right(d, k).wait_send())
+            pl.when(sends_left(d))(lambda d=d: to_left(d, k).wait_send())
+
+    for step in range(1, MODEL):
+        square_copy(step).wait_send()
+    for j in range(pieces):
+        core_copy(j).wait_send()
+        x_copy(j).wait_send()
+        for step in range(1, BATCH):
+            z_copy(j, step).wait_send()
+
+
+def fused_device(tokens, norm_gain, w_qkv, key_cache, value_cache, lengths):
+    features, width = w_qkv.shape
+    chunks = features // CHUNK
+    pieces = width // PIECE_COLS
+    dma = pltpu.SemaphoreType.DMA
+    vmem = pl.BlockSpec(memory_space=pltpu.VMEM)
+    hbm = pl.BlockSpec(memory_space=pl.ANY)
+    hops = BATCH - 1
+    context = pl.pallas_call(
+        fused_kernel,
+        out_shape=jax.ShapeDtypeStruct((SHARE, HQ, HD), jnp.bfloat16),
+        in_specs=[pl.BlockSpec(memory_space=pltpu.SMEM), vmem, vmem, hbm, hbm, hbm],
+        out_specs=vmem,
+        scratch_shapes=[
+            pltpu.VMEM((chunks, CHUNK, width), jnp.bfloat16),
+            pltpu.VMEM(key_cache.shape, jnp.bfloat16),
+            pltpu.VMEM(value_cache.shape, jnp.bfloat16),
+            pltpu.VMEM((chunks, BATCH, 2 * ROWS, HALF), jnp.bfloat16),
+            pltpu.VMEM((2 * BATCH * ROWS, 2 * BATCH * ROWS), jnp.bfloat16),
+            pltpu.VMEM((BATCH * PIECE_ROWS, LANES), jnp.bfloat16),
+            pltpu.VMEM((SHARE, 2 * HEAD_ROWS, BATCH * pieces * PIECE_ROWS), jnp.bfloat16),
+            pltpu.VMEM((BATCH * ROWS, width), jnp.float32),
+            pltpu.VMEM((pieces, 2 * ROWS, PIECE_COLS), jnp.float32),
+            pltpu.VMEM((pieces, ROWS, PIECE_COLS), jnp.float32),
+            pltpu.VMEM((pieces, ROWS, PIECE_COLS), jnp.float32),
+            pltpu.VMEM((pieces, BATCH, PIECE_ROWS, LANES), jnp.bfloat16),
+            pltpu.VMEM((BATCH, pieces, PIECE_ROWS, LANES), jnp.bfloat16),
+            pltpu.VMEM((MODEL, ROWS, LANES), jnp.float32),
+            pltpu.VMEM((ROWS, LANES), jnp.float32),
+            dma((chunks,)), dma((2,)),
+            dma((hops, chunks)), dma((hops, chunks)), dma((hops, chunks)), dma((hops, chunks)),
+            dma((pieces,)), dma((pieces,)), dma((pieces,)), dma((pieces,)),
+            dma((BATCH, pieces)), dma((BATCH, pieces)),
+            dma((MODEL,)), dma((MODEL,)),
+        ],
+        compiler_params=pltpu.CompilerParams(
+            collective_id=0, has_side_effects=True, vmem_limit_bytes=54 * 1024 * 1024
+        ),
+        name="qkv_attention",
+    )(lengths, tokens, norm_gain.reshape(1, features), w_qkv, key_cache, value_cache)
+    return context.reshape(SHARE, HQ * HD)
+
+
+def per_device(tokens, norm_gain, w_qkv, key_cache, value_cache, lengths):
+    fits = (
+        lax.axis_size("batch") == BATCH
+        and lax.axis_size("mp") == MODEL
+        and tokens.shape[0] == ROWS
+        and w_qkv.shape[0] % CHUNK == 0
+        and w_qkv.shape[1] % PIECE_COLS == 0
+        and w_qkv.shape[1] * BATCH == (HQ + 2) * HD
+    )
+    run = fused_device if fits else plain_device
+    return run(tokens, norm_gain, w_qkv, key_cache, value_cache, lengths)
 
 
 def solution(mesh):

time: 84.4 us -> 51.9 us (0.61)
  blocking collectives: 50.1 us -> 0 us
  Pallas kernels: 0 us -> 48.7 us
  matrix products: 14.1 us -> 0 us
  waiting for transfers between devices: 7.75 us -> 0 us
  starting transfers between devices: 3.37 us -> 0 us
  local copies, waits for them, and re-layouts: 6.21 us -> 2.98 us
  other arithmetic: 2.37 us -> 0 us
    pallas_call x0 -> x1, Pallas kernels: none -> 48.7 us  [fused_device(): pl.pallas_call(fused_kernel, out_shape=jax.ShapeDtypeStruct((SHARE, HQ, H...]
    unnamed x1 -> x0, blocking collectives: 27.7 us -> none
    all_gather x1 -> x0, blocking collectives: 22.4 us -> none  [per_device(): lax.all_gather(normed, 'batch', axis=0, tiled=True)]
    dot_general x4 -> x0, matrix products: 14.1 us -> none  [the longest x1 12.9 us: per_device(): jnp.dot(lax.all_gather(normed, 'batch', axis=0, tiled=True), w_qkv, prefe...]
    all_to_all x1 -> x0, waiting for transfers between devices: 7.75 us -> none  [per_device(): lax.all_to_all(summed.astype(jnp.bfloat16), 'batch', split_axis=0, concat...]
    all_to_all x1 -> x0, starting transfers between devices: 3.37 us -> none  [per_device(): lax.all_to_all(summed.astype(jnp.bfloat16), 'batch', split_axis=0, concat...]
    reshape x3 -> x1, local copies, waits for them, and re-layouts: 3.29 us -> 1.35 us  [fused_device(): norm_gain.reshape(1, features)]
    convert_element_type x2 -> x0, local copies, waits for them, and re-layouts: 1.4 us -> none  [per_device(): summed.astype(jnp.bfloat16)]
  transfers between devices with their start and end apart: 1 -> 0, of which waited for: 1 -> 0; matrix products, arithmetic and copies ran while one was open for 1% -> 0% of each run, Pallas kernels for 0% -> 0%
where the time goes in v1:
time: 51.9 us; the launch traced here: 51.7 us
  Pallas kernels  48.7 us (94%)
  local copies, waits for them, and re-layouts  2.98 us (6%)
    pallas_call x1, Pallas kernels, fused_device(): pl.pallas_call(fused_kernel, out_shape=jax.ShapeDtypeStruct((SHARE, HQ, H...  48.7 us
    unnamed x1, local copies, waits for them, and re-layouts  1.63 us
    reshape x1, local copies, waits for them, and re-layouts, fused_device(): norm_gain.reshape(1, features)  1.35 us

profile of v1, /device:TPU:0, one launch (start us, length us, event | category | flops | bytes accessed | tf_op | source)
XLA Modules:
  0.0 51.7 jit_solution(6823823718652330230)
XLA Ops:
  0.0 1.3 %reshape.6.gain_ref = f32[1,4608]{1,0:T(1,128)} reshape(f32[4608]{0:T(1024)} %param.7) | data formatting | bytes 36864 | tf_op jit(solution)/shard_map/reshape | solution.py:448
  1.3 48.7 %qkv_attention.1 = bf16[6,48,256]{2,1,0:T(8,128)(2,1)} custom-call(s32[6]{0:T(128)} %lengths_ref.1, bf16[24,4608]{1,0:T(8,128)(2,1)} %tokens_ref.1, f32[1,4608]{1,0:T(1,128)} %reshape.6.gain_ref, bf16[4608,3200]{1,0:T(8,128)(2,1)} %w_ref.1, bf16[6,512,256]{2,1,0:T(8,128)(2,1)} %key_ref.1, bf16[6,512,256]{2,1,0:T(8,128)(2,1)} %value_ref.1), custom_call_target="tpu_custom_call" | custom-call | tf_op jit(solution)/shard_map/qkv_attention/pallas_call | solution.py:417
  50.0 1.6 %copy.7 = bf16[1,6,48,256]{3,1,2,0:T(8,128)(2,1)} copy(bf16[1,6,48,256]{3,2,1,0:T(8,128)(2,1)} %bitcast.2) | data formatting | bytes 294912

commit v2 on v1

--- a/solution.py
+++ b/solution.py
@@ -26,6 +26,8 @@
 PIECE_COLS = PIECE * LANES
 PIECE_ROWS = 32
 HEAD_ROWS = 64
+AHEAD = 4
+LAG = 3
 MESH_ID = pl.DeviceIdType.MESH
 
 
@@ -184,7 +186,7 @@
         for half in range(2):
             columns = pl.ds(k * CHUNK + half * HALF, HALF)
             widened = tokens_ref[:, columns].astype(jnp.float32)
-            parts.append(widened * gain_ref[:, columns])
+            parts.append(widened * gain_ref[columns][None, :])
             squared = widened * widened
             total = total + squared[:, :LANES] + squared[:, LANES:]
         gathered[k, batch] = jnp.concatenate(parts, axis=0).astype(jnp.bfloat16)
@@ -241,8 +243,8 @@
             if d + 1 < BATCH - 1:
                 pl.when(batch > 0)(lambda: to_left(d + 1, k).start())
 
-    send(0, 0)
-    send(0, 1)
+    for k in range(AHEAD):
+        send(0, k)
 
     def square_copy(step):
         return pltpu.make_async_remote_copy(
@@ -270,15 +272,15 @@
     width = w_ref.shape[1]
     tile = 3 * HD
 
-    @pl.loop(0, chunks + 1)
+    @pl.loop(0, chunks - 1 + 2 * LAG)
     def _(it):
-        pl.when(it + 2 < chunks)(lambda: send(0, it + 2))
+        pl.when(it + AHEAD < chunks)(lambda: send(0, it + AHEAD))
         pl.when(it < chunks)(lambda: receive(0, it))
-        pl.when(jnp.logical_and(it >= 1, it < chunks + 1))(lambda: receive(1, it - 1))
-
-        @pl.when(it >= 2)
+        pl.when(jnp.logical_and(it >= LAG, it < chunks + LAG))(lambda: receive(1, it - LAG))
+
+        @pl.when(it >= 2 * LAG)
         def _():
-            k = it - 2
+            k = it - 2 * LAG
             receive(2, k)
             w_copy(k).wait()
             left = left_side(k)
@@ -445,7 +447,7 @@
             collective_id=0, has_side_effects=True, vmem_limit_bytes=54 * 1024 * 1024
         ),
         name="qkv_attention",
-    )(lengths, tokens, norm_gain.reshape(1, features), w_qkv, key_cache, value_cache)
+    )(lengths, tokens, norm_gain, w_qkv, key_cache, value_cache)
     return context.reshape(SHARE, HQ * HD)
 
 

time: 51.9 us -> 44.2 us (0.85)
  Pallas kernels: 48.7 us -> 42.4 us
  local copies, waits for them, and re-layouts: 2.98 us -> 1.63 us
    pallas_call x1, Pallas kernels: 48.7 us -> 42.4 us  [fused_device(): pl.pallas_call(fused_kernel, out_shape=jax.ShapeDtypeStruct((SHARE, HQ, H...]
    reshape x1 -> x0, local copies, waits for them, and re-layouts: 1.35 us -> none  [fused_device(): norm_gain.reshape(1, features)]
where the time goes in v2:
time: 44.2 us; the launch traced here: 44.1 us
  Pallas kernels  42.4 us (96%)
  local copies, waits for them, and re-layouts  1.63 us (4%)
    pallas_call x1, Pallas kernels, fused_device(): pl.pallas_call(fused_kernel, out_shape=jax.ShapeDtypeStruct((SHARE, HQ, H...  42.4 us
    unnamed x1, local copies, waits for them, and re-layouts  1.63 us

profile of v2, /device:TPU:0, one launch (start us, length us, event | category | flops | bytes accessed | tf_op | source)
XLA Modules:
  0.0 44.1 jit_solution(13721315128423248244)
XLA Ops:
  0.0 42.4 %qkv_attention.1 = bf16[6,48,256]{2,1,0:T(8,128)(2,1)} custom-call(s32[6]{0:T(128)} %lengths_ref.1, bf16[24,4608]{1,0:T(8,128)(2,1)} %tokens_ref.1, f32[4608]{0:T(1024)} %gain_ref.1, bf16[4608,3200]{1,0:T(8,128)(2,1)} %w_ref.1, bf16[6,512,256]{2,1,0:T(8,128)(2,1)} %key_ref.1, bf16[6,512,256]{2,1,0:T(8,128)(2,1)} %value_ref.1), custom_call_target="tpu_custom_call" | custom-call | tf_op jit(solution)/shard_map/qkv_attention/pallas_call | solution.py:419
  42.4 1.6 %copy.7 = bf16[1,6,48,256]{3,1,2,0:T(8,128)(2,1)} copy(bf16[1,6,48,256]{3,2,1,0:T(8,128)(2,1)} %bitcast.2) | data formatting | bytes 294912

commit v3 on v2

--- a/solution.py
+++ b/solution.py
@@ -28,6 +28,7 @@
 HEAD_ROWS = 64
 AHEAD = 4
 LAG = 3
+TOGETHER = 3
 MESH_ID = pl.DeviceIdType.MESH
 
 
@@ -367,7 +368,8 @@
 
     columns = z_in[...].reshape(BATCH * pieces * PIECE_ROWS, LANES)
     positions = lax.broadcasted_iota(jnp.int32, (HQ, key_ref.shape[1]), 1)
-    for row in range(SHARE):
+
+    def score(row):
         picked = jnp.dot(heads[row], columns, preferred_element_type=jnp.float32)
         joined = jnp.concatenate([picked[:HEAD_ROWS], picked[HEAD_ROWS:]], axis=1)
         queries = joined[:HQ]
@@ -381,17 +383,30 @@
         own_score = jnp.sum(queries * new_key, axis=1, keepdims=True) * (
             inv_rms * inv_rms / math.sqrt(HD)
         )
+        return scores, own_score, inv_rms * new_value
+
+    def soften(row, scores, own_score):
         valid = positions < lengths_ref[row]
         scores = jnp.where(valid, scores, NEG_FILL)
         row_max = jnp.maximum(jnp.max(scores, axis=1, keepdims=True), own_score)
         weights = jnp.where(valid, jnp.exp(scores - row_max), 0.0)
         own_weight = jnp.exp(own_score - row_max)
         denominator = jnp.sum(weights, axis=1, keepdims=True) + own_weight
-        weighted = jnp.dot(
-            weights.astype(jnp.bfloat16), value_buf[row], preferred_element_type=jnp.float32
-        )
-        weighted = weighted + own_weight * inv_rms * new_value
-        out_ref[row] = (weighted / denominator).astype(jnp.bfloat16)
+        return weights.astype(jnp.bfloat16), own_weight, denominator
+
+    def combine(row, weights_low, own_weight, denominator, own_value):
+        weighted = jnp.dot(weights_low, value_buf[row], preferred_element_type=jnp.float32)
+        return ((weighted + own_weight * own_value) / denominator).astype(jnp.bfloat16)
+
+    for first in range(0, SHARE, TOGETHER):
+        rows = range(first, first + TOGETHER)
+        scored = [score(row) for row in rows]
+        softened = [soften(row, *scored[row - first][:2]) for row in rows]
+        contexts = [
+            combine(row, *softened[row - first], scored[row - first][2]) for row in rows
+        ]
+        for row in rows:
+            out_ref[row] = contexts[row - first]
 
     @pl.loop(0, chunks)
     def _(k):

time: 44.2 us -> 43.2 us (0.977)
  Pallas kernels: 42.4 us -> 41.4 us
    pallas_call x1, Pallas kernels: 42.4 us -> 41.4 us  [fused_device(): pl.pallas_call(fused_kernel, out_shape=jax.ShapeDtypeStruct((SHARE, HQ, H...]
where the time goes in v3:
time: 43.2 us; the launch traced here: 43.1 us
  Pallas kernels  41.4 us (96%)
  local copies, waits for them, and re-layouts  1.63 us (4%)
    pallas_call x1, Pallas kernels, fused_device(): pl.pallas_call(fused_kernel, out_shape=jax.ShapeDtypeStruct((SHARE, HQ, H...  41.4 us
    unnamed x1, local copies, waits for them, and re-layouts  1.63 us

profile of v3, /device:TPU:0, one launch (start us, length us, event | category | flops | bytes accessed | tf_op | source)
XLA Modules:
  0.0 43.1 jit_solution(13729262320658142489)
XLA Ops:
  0.0 41.4 %qkv_attention.1 = bf16[6,48,256]{2,1,0:T(8,128)(2,1)} custom-call(s32[6]{0:T(128)} %lengths_ref.1, bf16[24,4608]{1,0:T(8,128)(2,1)} %tokens_ref.1, f32[4608]{0:T(1024)} %gain_ref.1, bf16[4608,3200]{1,0:T(8,128)(2,1)} %w_ref.1, bf16[6,512,256]{2,1,0:T(8,128)(2,1)} %key_ref.1, bf16[6,512,256]{2,1,0:T(8,128)(2,1)} %value_ref.1), custom_call_target="tpu_custom_call" | custom-call | tf_op jit(solution)/shard_map/qkv_attention/pallas_call | solution.py:434
  41.4 1.6 %copy.7 = bf16[1,6,48,256]{3,1,2,0:T(8,128)(2,1)} copy(bf16[1,6,48,256]{3,2,1,0:T(8,128)(2,1)} %bitcast.2) | data formatting | bytes 294912

commit v4 on v3

--- a/solution.py
+++ b/solution.py
@@ -19,15 +19,15 @@
 MODEL = 4
 ROWS = 24
 SHARE = 6
-HALF = 256
+HALF = 384
 CHUNK = 2 * HALF
 LANES = 128
 PIECE = 5
 PIECE_COLS = PIECE * LANES
 PIECE_ROWS = 32
 HEAD_ROWS = 64
-AHEAD = 4
-LAG = 3
+AHEAD = 3
+LAG = 2
 TOGETHER = 3
 MESH_ID = pl.DeviceIdType.MESH
 
@@ -189,7 +189,8 @@
             widened = tokens_ref[:, columns].astype(jnp.float32)
             parts.append(widened * gain_ref[columns][None, :])
             squared = widened * widened
-            total = total + squared[:, :LANES] + squared[:, LANES:]
+            for start in range(0, HALF, LANES):
+                total = total + squared[:, start : start + LANES]
         gathered[k, batch] = jnp.concatenate(parts, axis=0).astype(jnp.bfloat16)
     squares[model] = jnp.broadcast_to(jnp.sum(total, axis=1, keepdims=True), (ROWS, LANES))
 

time: 43.2 us -> 42.2 us (0.977)
  Pallas kernels: 41.4 us -> 40.4 us
    pallas_call x1, Pallas kernels: 41.4 us -> 40.4 us  [fused_device(): pl.pallas_call(fused_kernel, out_shape=jax.ShapeDtypeStruct((SHARE, HQ, H...]
where the time goes in v4:
time: 42.2 us; the launch traced here: 42 us
  Pallas kernels  40.4 us (96%)
  local copies, waits for them, and re-layouts  1.63 us (4%)
    pallas_call x1, Pallas kernels, fused_device(): pl.pallas_call(fused_kernel, out_shape=jax.ShapeDtypeStruct((SHARE, HQ, H...  40.4 us
    unnamed x1, local copies, waits for them, and re-layouts  1.63 us

profile of v4, /device:TPU:0, one launch (start us, length us, event | category | flops | bytes accessed | tf_op | source)
XLA Modules:
  0.0 42.0 jit_solution(15968150717826913899)
XLA Ops:
  0.0 40.4 %qkv_attention.1 = bf16[6,48,256]{2,1,0:T(8,128)(2,1)} custom-call(s32[6]{0:T(128)} %lengths_ref.1, bf16[24,4608]{1,0:T(8,128)(2,1)} %tokens_ref.1, f32[4608]{0:T(1024)} %gain_ref.1, bf16[4608,3200]{1,0:T(8,128)(2,1)} %w_ref.1, bf16[6,512,256]{2,1,0:T(8,128)(2,1)} %key_ref.1, bf16[6,512,256]{2,1,0:T(8,128)(2,1)} %value_ref.1), custom_call_target="tpu_custom_call" | custom-call | tf_op jit(solution)/shard_map/qkv_attention/pallas_call | solution.py:435
  40.4 1.6 %copy.7 = bf16[1,6,48,256]{3,1,2,0:T(8,128)(2,1)} copy(bf16[1,6,48,256]{3,2,1,0:T(8,128)(2,1)} %bitcast.2) | data formatting | bytes 294912
